TPU v7x, 32 devices: a whole 2x2x4 slice. The times are simulated.
32 devices in a mesh: groups: 2 (over x), srow: 8 (over z, y), scol: 2 (over core).
Axes of the slice: x: 2, y: 2, z: 4, core: 2. Of those that a mesh axis runs over, the one named last changes fastest.
Arguments:
- field_in: bfloat16 [256, 4096], P(('groups', 'srow'), 'scol'), parts along dimension 0, may hold values from -6 to 6
- cotangent: bfloat16 [256, 4096], P('groups', 'srow'), parts along dimension 0, may hold values from -6 to 6
- tile_vals: bfloat16 [16, 64, 128, 128], P(('groups', 'srow'), 'scol'), parts along dimension 0, may hold values from -0.1875 to 0.1875
- tile_rows: int32 [16, 64], P(('groups', 'srow'), 'scol'), parts along dimension 0, may hold values from 0 to 31, as said below
- tile_cols: int32 [16, 64], P('groups', 'scol'), parts along dimension 0, may hold values from 0 to 31, as said below
- lag_steps: int32 [4], P('groups'), parts along dimension 0, may hold values from 1 to 24, as said below
- ar_coef: float32 [6, 128], P('groups'), parts along dimension 0, may hold values from -1 to 1
Outputs:
- forward_out: float32 [256, 4096], P(('groups', 'scol'), 'srow'), parts along dimension 0
- adjoint_out: float32 [256, 4096], P(('groups', 'srow'), 'scol'), parts along dimension 0
There are 2 independent parts, one for each index of `groups`. A program takes and returns all parts, laid end to end along the dimension named above; each array names one. Nothing has to cross between parts.
Inputs may be any that keep to these rules, and one draw needn't show every extreme that they name: `tile_rows`: the tiles of device (r, c), entries [r, c * 32] to [r, c * 32 + 31], lie in row blocks r * 4 to r * 4 + 3, each such row block holding exactly 8 of them. `tile_cols`: entries [., c * 32 + k] lie in column blocks c * 16 to c * 16 + 15; every column block has at least one tile. lag_steps[0] < lag_steps[1] = 24.
All inputs are finite; a program needn't handle non-finite values.
Results may differ from a plain program's by a relative error of at most 0.0029.
Values may be sent and summed in bfloat16 or wider, within the bound.
A program may use at most 128 MiB of HBM per device.

v0:
```python
import jax
import jax.numpy as jnp
from jax import lax
from jax.sharding import PartitionSpec as P

BS = 128
RBD = 4
TD = 16
MAXLAG = 24


def passed_along(value, axis, by):
    size = lax.axis_size(axis)
    pairs = [(i, i + by) for i in range(size) if 0 <= i + by < size]
    return lax.ppermute(value, axis, pairs)


def body(field_in, cotangent, tile_vals, tile_rows, tile_cols, lag_steps, ar_coef):
    row_index = lax.axis_index("srow")
    col_index = lax.axis_index("scol")
    tile_mats = tile_vals[0]
    col_blocks = field_in.shape[1] // BS
    row_local = tile_rows[0] - row_index * RBD
    all_cols = tile_cols - col_index * col_blocks
    own_cols = lax.dynamic_slice_in_dim(all_cols, row_index, 1, 0)[0]
    blocks = field_in.reshape(field_in.shape[0], col_blocks, BS)
    outgoing = jnp.take(blocks, all_cols.reshape(-1), axis=1)
    picked = lax.all_to_all(outgoing, "srow", split_axis=1, concat_axis=0, tiled=True)
    products = jnp.einsum("tkd,ked->tke", picked, tile_mats, preferred_element_type=jnp.float32)
    summed = jnp.zeros((picked.shape[0], RBD, BS), jnp.float32).at[:, row_local].add(products)
    partial_value = summed.reshape(picked.shape[0], RBD * BS)
    space_image = lax.psum_scatter(partial_value, "scol", scatter_dimension=0, tiled=True).astype(
        jnp.bfloat16
    )
    half_rows = space_image.shape[0]
    earlier = passed_along(space_image[half_rows - MAXLAG :], "scol", 1)
    extended = jnp.concatenate([earlier, space_image], 0).astype(jnp.float32)
    coef_half = lax.dynamic_slice_in_dim(ar_coef, col_index * half_rows, half_rows, 1)

    def delayed(lag):
        return lax.dynamic_slice_in_dim(extended, MAXLAG - lag, half_rows, 0)

    forward_out = (
        coef_half[0][:, None] * extended[MAXLAG:]
        + coef_half[1][:, None] * delayed(lag_steps[0])
        + coef_half[2][:, None] * delayed(lag_steps[1])
    )
    cot_wide = cotangent.astype(jnp.float32)
    hours_all = cot_wide.shape[0]
    padding = jnp.zeros((MAXLAG, cot_wide.shape[1]), jnp.float32)

    def advanced(values, lag):
        padded = jnp.concatenate([values, padding], 0)
        return lax.dynamic_slice_in_dim(padded, lag, hours_all, 0)

    time_adjoint = (
        ar_coef[0][:, None] * cot_wide
        + advanced(ar_coef[1][:, None] * cot_wide, lag_steps[0])
        + advanced(ar_coef[2][:, None] * cot_wide, lag_steps[1])
    ).astype(jnp.bfloat16)
    row_picked = jnp.take(time_adjoint.reshape(hours_all, RBD, BS), row_local, axis=1)
    products = jnp.einsum("tke,ked->tkd", row_picked, tile_mats, preferred_element_type=jnp.float32)
    summed = (
        jnp.zeros((TD * lax.axis_size("srow"), col_blocks, BS), jnp.float32)
        .at[:, own_cols]
        .add(products)
    )
    adjoint_out = lax.psum_scatter(
        summed.reshape(TD * lax.axis_size("srow"), col_blocks * BS),
        "srow",
        scatter_dimension=0,
        tiled=True,
    )
    return (forward_out, adjoint_out)


def solution(mesh):
    in_specs = (
        P(("groups", "srow"), "scol"),
        P("groups", "srow"),
        P(("groups", "srow"), "scol", None, None),
        P(("groups", "srow"), "scol"),
        P("groups", "scol"),
        P("groups"),
        P("groups", None),
    )
    out_specs = (P(("groups", "scol"), "srow"), P(("groups", "srow"), "scol"))
    return jax.shard_map(body, mesh=mesh, in_specs=in_specs, out_specs=out_specs, check_vma=False)
```

profile of v0, /device:TPU:0, one launch (start us, length us, event | category | flops | bytes accessed | tf_op | source)
XLA Modules:
  0.0 132.2 jit_solution(7455118790495822102)
XLA Ops:
  7.2 0.0 copy-start
  7.2 0.8 broadcast_subtract_fusion
  8.0 0.1 reshape.120
  8.0 0.1 reshape.118
  8.1 0.9 copy_bitcast_fusion
  9.0 0.9 gather_fusion
  9.9 0.0 copy-start.3
  9.9 0.0 copy-start.1
  9.9 0.0 copy-start.2
  9.9 1.7 %select_bitcast_fusion = bf16[16,256,128]{2,0,1:T(8,128)(2,1)} fusion(bf16[256,16,128]{2,1,0:T(8,128)(2,1)S(1)} %gather_fusion, pred[256]{0:T(512)(128)(4,1)S(1)} %compare_and_fusion.1), kind=kLoop, calls=%fused_computation.10 | loop fusion | flops 524288 | bytes 2097408 | tf_op jit(solution)/shard_map/jit(_take)/select_n | solution.py:27
  11.6 0.0 copy-start.4
  11.6 7.4 %all-to-all-start = ((bf16[16,256,128]{2,0,1:T(8,128)(2,1)}), bf16[16,256,128]{2,0,1:T(8,128)(2,1)S(1)}, u32[]{:S(2)}, u32[]{:S(2)}) async-start(bf16[16,256,128]{2,0,1:T(8,128)(2,1)} %select_bitcast_fusion), calls=%async_computation | async-start | bytes 2097152 | tf_op jit(solution)/shard_map/all_to_all | solution.py:28
  19.0 0.0 reduce-scatter.7.cloned.1.call-start
  19.1 0.0 copy-done.3
  19.1 0.6 fusion.17
  22.1 0.0 copy-done.1
  22.1 0.1 copy.28
  23.4 0.0 copy-done.2
  23.5 0.2 fusion.10
  23.7 0.1 copy.29
  23.9 0.0 copy-done.4
  23.9 1.7 %gather_fusion.1 = bf16[32,128,128]{2,1,0:T(8,128)(2,1)} fusion(bf16[128,4,128]{2,0,1:T(8,128)(2,1)S(1)} %copy.29, s32[1024]{0:T(1024)S(1)} %pad_clamp_fusion), kind=kCustom, calls=%fused_computation.1 | custom fusion | bytes 2097280 | tf_op jit(solution)/shard_map/jit(_take)/gather | solution.py:61
  25.6 19.2 %all-to-all-done = bf16[16,256,128]{2,0,1:T(8,128)(2,1)S(1)} async-done(((bf16[16,256,128]{2,0,1:T(8,128)(2,1)}), bf16[16,256,128]{2,0,1:T(8,128)(2,1)S(1)}, u32[]{:S(2)}, u32[]{:S(2)}) %all-to-all-start) | async-done | bytes 1048608 | tf_op jit(solution)/shard_map/all_to_all | solution.py:28
  44.8 0.3 copy.26
  45.1 0.0 copy-done
  45.1 0.9 fusion.3
  46.0 2.7 %scatter_fusion = f32[128,4,128]{2,0,1:T(8,128)S(1)} fusion(f32[128,4,128]{2,0,1:T(8,128)S(1)} %broadcast_in_dim.29, s32[32]{0:T(128)S(1)} %get-tuple-element.18, f32[32,128,128]{2,1,0:T(8,128)S(1)} %fusion.3), kind=kCustom, calls=%fused_computation.2 | custom fusion | flops 524288 | bytes 6291584 | tf_op jit(solution)/shard_map/scatter-add | solution.py:30
  48.6 0.1 copy.27
  48.8 0.8 copy.34
  49.6 0.0 reduce-scatter.7.cloned.1.call-update
  49.6 0.0 reduce-scatter.9.cloned.1.call-start
  49.7 3.1 %fusion = f32[32,128,128]{2,1,0:T(8,128)} fusion(bf16[1,32,128,128]{3,2,1,0:T(8,128)(2,1)S(1)} %copy-done, bf16[32,128,128]{2,1,0:T(8,128)(2,1)} %gather_fusion.1, pred[32]{0:T(512)(128)(4,1)S(1)} %compare_and_fusion), kind=kOutput, calls=%fused_computation.4 | convolution fusion | flops 134742016 | bytes 4194336 | tf_op jit(solution)/shard_map/tke,ked->tkd/dot_general | solution.py:62
  52.8 0.1 broadcast_in_dim.32
  52.9 4.7 %scatter_fusion.1 = f32[128,16,128]{2,0,1:T(8,128)S(1)} fusion(f32[128,16,128]{2,0,1:T(8,128)S(1)} %broadcast_in_dim.32, s32[32]{0:T(128)S(1)} %get-tuple-element.19, f32[32,128,128]{2,1,0:T(8,128)} %fusion), kind=kCustom, calls=%fused_computation.3 | custom fusion | flops 524288 | bytes 6291584 | tf_op jit(solution)/shard_map/scatter-add | solution.py:66
  57.6 0.3 copy.30
  57.9 1.3 copy.36
  59.2 0.0 reduce-scatter.9.cloned.1.call-update
  59.2 0.1 constant_dynamic-slice_fusion.1
  59.3 0.0 reduce-scatter.7.cloned.1.call-done
  59.3 1.0 copy.35
  60.4 0.1 slice.46
  60.5 1.3 collective-permute-start
  64.2 0.0 collective-permute-done
  64.2 0.1 maximum_convert_fusion
  64.3 0.3 fusion.12
  64.6 0.8 copy.31
  65.4 60.0 %reduce-scatter.9.cloned.1.call-done = f32[16,2048]{1,0:T(8,128)} async-done(((f32[128,2048]{1,0:T(8,128)}), f32[16,2048]{1,0:T(8,128)}) %reduce-scatter.9.cloned.1.call-update) | async-done | bytes 131088
  (10 shorter events, 0.1 us)
Async XLA Ops:
  7.2 37.9 %copy-start = (bf16[1,32,128,128]{3,2,1,0:T(8,128)(2,1)S(1)}, bf16[1,32,128,128]{3,2,1,0:T(8,128)(2,1)}, u32[]{:S(2)}) copy-start(bf16[1,32,128,128]{3,2,1,0:T(8,128)(2,1)} %param.9) | copy-start | bytes 3145732
  9.9 9.2 %copy-start.3 = (s32[2]{0:T(128)S(1)}, s32[2]{0:T(128)}, u32[]{:S(2)}) copy-start(s32[2]{0:T(128)} %param.12) | copy-start | bytes 28
  9.9 12.2 %copy-start.1 = (bf16[128,512]{1,0:T(8,128)(2,1)S(1)}, bf16[128,512]{1,0:T(8,128)(2,1)}, u32[]{:S(2)}) copy-start(bf16[128,512]{1,0:T(8,128)(2,1)} %param.8) | copy-start | bytes 393220
  9.9 13.5 %copy-start.2 = (f32[3,128]{1,0:T(4,128)S(1)}, f32[3,128]{1,0:T(4,128)}, u32[]{:S(2)}) copy-start(f32[3,128]{1,0:T(4,128)} %param.13) | copy-start | bytes 4612
  11.6 12.2 %copy-start.4 = (s32[1,32]{1,0:T(1,128)S(1)}, s32[1,32]{1,0:T(1,128)}, u32[]{:S(2)}) copy-start(s32[1,32]{1,0:T(1,128)} %param.10) | copy-start | bytes 388
  11.6 33.2 %all-to-all-start = ((bf16[16,256,128]{2,0,1:T(8,128)(2,1)}), bf16[16,256,128]{2,0,1:T(8,128)(2,1)S(1)}, u32[]{:S(2)}, u32[]{:S(2)}) async-start(bf16[16,256,128]{2,0,1:T(8,128)(2,1)} %select_bitcast_fusion), calls=%async_computation | async-start | bytes 2097152 | tf_op jit(solution)/shard_map/all_to_all | solution.py:28
  19.0 40.3 %reduce-scatter.7.cloned.1.call-start = ((), (), s32[]{:S(2)}) async-start(), calls=%async_computation.3 | async-start | bytes 393216
  49.6 75.7 %reduce-scatter.9.cloned.1.call-start = ((), (), s32[]{:S(2)}) async-start(), calls=%async_computation.4 | async-start | bytes 1179648
  60.5 3.7 %collective-permute-start = (bf16[24,512]{0,1:T(8,128)(2,1)S(1)}, bf16[24,512]{0,1:T(8,128)(2,1)S(1)}, u32[]{:S(2)}, u32[]{:S(2)}) collective-permute-start(bf16[24,512]{0,1:T(8,128)(2,1)S(1)} %slice.46), channel_id=1, source_target_pairs={{0,1},{2,3},{4,5},{6,7},{8,9},{10,11},{12,13},{14,15},{16,17},{18,... | collective-permute-start | bytes 73736 | tf_op jit(solution)/shard_map/ppermute | solution.py:15
Sparse Core Ops, SparseCore 0:
  49.8 6.6 reduce-scatter.6
  60.8 64.4 reduce-scatter.8
where the time goes:
time: 133 us; the launch traced here: 132 us
  waiting for transfers between devices  79.2 us (60%)
  between operations  20.3 us (15%)
  other arithmetic  10.5 us (8%)
  local copies, waits for them, and re-layouts  9.37 us (7%)
  starting transfers between devices  8.79 us (7%)
  matrix products  3.92 us (3%)
    unnamed x4, waiting for transfers between devices  60 us
    all_to_all x1, waiting for transfers between devices, body(): lax.all_to_all(outgoing, 'srow', split_axis=1, concat_axis=0, tiled=True)  19.2 us
    all_to_all x1, starting transfers between devices, body(): lax.all_to_all(outgoing, 'srow', split_axis=1, concat_axis=0, tiled=True)  7.41 us
    scatter-add x1, other arithmetic, body(): summed = jnp.zeros((TD * lax.axis_size('srow'), col_blocks, BS), jnp.floa...  4.7 us
    unnamed x15, local copies, waits for them, and re-layouts  4.08 us
    dot_general x1, matrix products, body(): jnp.einsum('tke,ked->tkd', row_picked, tile_mats, preferred_element_type=...  3.07 us
  transfers between devices with their start and end apart: 4, of which 2 were waited for; matrix products, arithmetic and copies ran while one was open for 11% of the time, Pallas kernels for 0%

commit v1 on v0

v1 whole, which is shorter than its diff:
```python
import functools

import jax
import jax.numpy as jnp
from jax import lax
from jax.experimental import pallas as pl
from jax.experimental.pallas import tpu as pltpu
from jax.sharding import PartitionSpec as P

BS = 128
RBD = 4
TD = 16
MAXLAG = 24
F32 = jnp.float32
BF16 = jnp.bfloat16
MESH = pl.DeviceIdType.MESH


def shift_matrix(rows, cols, lag):
    at = lax.broadcasted_iota(jnp.int32, (rows, cols), 0) + lag
    return (lax.broadcasted_iota(jnp.int32, (rows, cols), 1) == at).astype(F32).astype(BF16)


def kernel(
    n,
    tiles,
    ncb,
    idx,
    coef,
    field,
    cot,
    mats,
    fwd_out,
    adj_out,
    field_all,
    field_v,
    field_send,
    cot_v,
    mats_v,
    adj_in,
    sums,
    adj_send,
    adj_recv,
    part,
    part_recv,
    local_sem,
    fs_sem,
    fr_sem,
    as_sem,
    ar_sem,
    ps_sem,
    pr_sem,
):
    hours = n * TD
    half = hours // 2
    ext = half + MAXLAG
    me = lax.axis_index("srow")
    mc = lax.axis_index("scol")
    o_row, o_col, o_prow, o_pcol = 0, tiles, 2 * tiles, 3 * tiles
    o_lrow = 4 * tiles
    o_lcol = o_lrow + RBD
    o_lag = o_lcol + ncb

    load_cot = pltpu.make_async_copy(cot, cot_v, local_sem.at[0])
    load_mats = pltpu.make_async_copy(mats, mats_v, local_sem.at[1])
    load_cot.start()
    load_mats.start()
    my_rows = pl.ds(pl.multiple_of(me * TD, TD), TD)
    load_own = pltpu.make_async_copy(field, field_v, local_sem.at[2])
    load_own.start()

    barrier = pltpu.get_barrier_semaphore()
    for i in range(1, n):
        pl.semaphore_signal(
            barrier, inc=1, device_id={"srow": lax.rem(me + i, n)}, device_id_type=MESH
        )
    pl.semaphore_signal(barrier, inc=1, device_id={"scol": 1 - mc}, device_id_type=MESH)
    load_own.wait()
    for b in range(ncb):
        block = field_v[:, b * BS : (b + 1) * BS]
        field_send[b] = block
        field_all[b, my_rows, :] = block
    pl.semaphore_wait(barrier, n)

    def rows_of(r):
        return pl.ds(pl.multiple_of(r * TD, TD), TD)

    def field_copy(dst, src):
        return pltpu.make_async_remote_copy(
            src_ref=field_send,
            dst_ref=field_all.at[:, rows_of(src), :],
            send_sem=fs_sem.at[dst],
            recv_sem=fr_sem.at[src],
            device_id={"srow": dst},
            device_id_type=MESH,
        )

    def adj_copy(dst, src):
        return pltpu.make_async_remote_copy(
            src_ref=adj_send.at[rows_of(dst), :],
            dst_ref=adj_recv.at[rows_of(src), :],
            send_sem=as_sem.at[dst],
            recv_sem=ar_sem.at[src],
            device_id={"srow": dst},
            device_id_type=MESH,
        )

    for i in range(1, n):
        field_copy(lax.rem(me + i, n), me).start()

    load_cot.wait()
    spread = coef[...]
    lag1 = idx[o_lag]
    early = cot_v[...]
    wide = early.astype(F32)
    later = jnp.dot(shift_matrix(hours, hours, lag1), early, preferred_element_type=F32)
    far = jnp.concatenate([wide[MAXLAG:], jnp.zeros((MAXLAG, RBD * BS), F32)], 0)
    adjoint = (
        spread[:, 0:1] * wide + spread[:, 3:4] * later + spread[:, 4:5] * far
    ).astype(BF16)
    for r in range(RBD):
        adj_in[r] = adjoint[:, r * BS : (r + 1) * BS]

    load_mats.wait()
    sums[0] = jnp.zeros((hours, BS), F32)

    def adj_step(k, carry):
        product = jnp.dot(adj_in[idx[o_row + k]], mats_v[k], preferred_element_type=F32)
        sums[k + 1] = sums[idx[o_pcol + k]] + product
        return carry

    lax.fori_loop(0, tiles, adj_step, 0, unroll=4)
    for b in range(ncb):
        adj_send[:, b * BS : (b + 1) * BS] = sums[idx[o_lcol + b]].astype(BF16)
    for i in range(1, n):
        adj_copy(lax.rem(me + i, n), me).start()

    for i in range(1, n):
        field_copy(me, lax.rem(me + n - i, n)).wait_recv()

    def fwd_step(k, carry):
        product = lax.dot_general(
            field_all[idx[o_col + k]], mats_v[k], (((1,), (1,)), ((), ())), preferred_element_type=F32
        )
        sums[k + 1] = sums[idx[o_prow + k]] + product
        return carry

    lax.fori_loop(0, tiles, fwd_step, 0, unroll=4)
    part[pl.ds(0, MAXLAG), :] = jnp.zeros((MAXLAG, RBD * BS), F32)
    for r in range(RBD):
        part[pl.ds(MAXLAG, hours), r * BS : (r + 1) * BS] = sums[idx[o_lrow + r]]
    exchange = pltpu.make_async_remote_copy(
        src_ref=part.at[pl.ds(pl.multiple_of((1 - mc) * half, 8), ext), :],
        dst_ref=part_recv,
        send_sem=ps_sem,
        recv_sem=pr_sem,
        device_id={"scol": 1 - mc},
        device_id_type=MESH,
    )
    exchange.start()
    exchange.wait_recv()
    own = part[pl.ds(pl.multiple_of(mc * half, 8), ext), :]
    value = (own + part_recv[...]).astype(BF16)
    spread = coef[pl.ds(pl.multiple_of(mc * half, 8), half), :]
    delayed = jnp.dot(
        shift_matrix(half, ext, MAXLAG - lag1), value, preferred_element_type=F32
    )
    value = value.astype(F32)
    fwd_out[...] = (
        spread[:, 0:1] * value[MAXLAG:] + spread[:, 1:2] * delayed + spread[:, 2:3] * value[:half]
    )

    adj_out[...] = adj_send[my_rows, :].astype(F32)
    for i in range(1, n):
        src = lax.rem(me + n - i, n)
        adj_copy(me, src).wait_recv()
        adj_out[...] += adj_recv[rows_of(src), :].astype(F32)

    exchange.wait_send()
    for i in range(1, n):
        dst = lax.rem(me + i, n)
        field_copy(dst, me).wait_send()
        adj_copy(dst, me).wait_send()


def body(field_in, cotangent, tile_vals, tile_rows, tile_cols, lag_steps, ar_coef):
    n = lax.axis_size("srow")
    row_index = lax.axis_index("srow")
    col_index = lax.axis_index("scol")
    tiles = tile_vals.shape[1]
    cols = field_in.shape[1]
    ncb = cols // BS
    hours = n * TD
    rows = tile_rows[0] - row_index * RBD
    own_cols = lax.dynamic_slice_in_dim(tile_cols, row_index, 1, 0)[0] - col_index * ncb
    place = jnp.arange(tiles, dtype=jnp.int32)
    earlier = place[None, :] < place[:, None]

    def chain(ids, blocks):
        same = (ids[:, None] == ids[None, :]) & earlier
        prev = jnp.max(jnp.where(same, place[None, :] + 1, 0), axis=1)
        which = jnp.arange(blocks, dtype=jnp.int32)[:, None] == ids[None, :]
        last = jnp.max(jnp.where(which, place[None, :] + 1, 0), axis=1)
        return prev, last

    prow, lrow = chain(rows, RBD)
    pcol, lcol = chain(own_cols, ncb)
    idx = jnp.concatenate([rows, own_cols, prow, pcol, lrow, lcol, lag_steps])
    padded = jnp.pad(ar_coef, ((0, 0), (0, MAXLAG)))
    ahead = lax.dynamic_slice_in_dim(padded[1], lag_steps[0], hours)
    spare = jnp.zeros((3, hours), F32)
    coef = jnp.concatenate([ar_coef, ahead[None], padded[2:3, MAXLAG:], spare]).T

    anyspace = pl.BlockSpec(memory_space=pl.ANY)
    vmem = pl.BlockSpec(memory_space=pltpu.VMEM)
    half = hours // 2
    wide = RBD * BS
    return pl.pallas_call(
        functools.partial(kernel, n, tiles, ncb),
        out_shape=(
            jax.ShapeDtypeStruct((half, wide), F32),
            jax.ShapeDtypeStruct((TD, cols), F32),
        ),
        in_specs=[pl.BlockSpec(memory_space=pltpu.SMEM), vmem, anyspace, anyspace, anyspace],
        out_specs=(vmem, vmem),
        scratch_shapes=[
            pltpu.VMEM((ncb, hours, BS), BF16),
            pltpu.VMEM((TD, cols), BF16),
            pltpu.VMEM((ncb, TD, BS), BF16),
            pltpu.VMEM((hours, wide), BF16),
            pltpu.VMEM((tiles, BS, BS), BF16),
            pltpu.VMEM((RBD, hours, BS), BF16),
            pltpu.VMEM((tiles + 1, hours, BS), F32),
            pltpu.VMEM((hours, cols), BF16),
            pltpu.VMEM((hours, cols), BF16),
            pltpu.VMEM((hours + MAXLAG, wide), F32),
            pltpu.VMEM((half + MAXLAG, wide), F32),
            pltpu.SemaphoreType.DMA((3,)),
            pltpu.SemaphoreType.DMA((n,)),
            pltpu.SemaphoreType.DMA((n,)),
            pltpu.SemaphoreType.DMA((n,)),
            pltpu.SemaphoreType.DMA((n,)),
            pltpu.SemaphoreType.DMA,
            pltpu.SemaphoreType.DMA,
        ],
        compiler_params=pltpu.CompilerParams(
            collective_id=0, has_side_effects=True, vmem_limit_bytes=58 * 1024 * 1024
        ),
        cost_estimate=pl.CostEstimate(
            flops=4 * tiles * hours * BS * BS, bytes_accessed=2 << 20, transcendentals=0
        ),
    )(idx, coef, field_in, cotangent, tile_vals[0])


def solution(mesh):
    in_specs = (
        P(("groups", "srow"), "scol"),
        P("groups", "srow"),
        P(("groups", "srow"), "scol", None, None),
        P(("groups", "srow"), "scol"),
        P("groups", "scol"),
        P("groups"),
        P("groups", None),
    )
    out_specs = (P(("groups", "scol"), "srow"), P(("groups", "srow"), "scol"))
    return jax.shard_map(body, mesh=mesh, in_specs=in_specs, out_specs=out_specs, check_vma=False)
```

time: 133 us -> 36.5 us (0.27)
  the two profiles are of different devices: /device:TPU:0 before, /device:TPU:13 now
where the time goes in v1:
time: 36.5 us; the launch traced here: 36.2 us
  Pallas kernels  29.1 us (80%)
  local copies, waits for them, and re-layouts  5.09 us (14%)
  other arithmetic  1.19 us (3%)
  between operations  0.8 us (2%)
    pallas_call x1, Pallas kernels, body(): pl.pallas_call(functools.partial(kernel, n, tiles, ncb), out_shape=(jax.S...  29.1 us
    unnamed x10, local copies, waits for them, and re-layouts  3.55 us
    concatenate x2, local copies, waits for them, and re-layouts, body(): jnp.concatenate([ar_coef, ahead[None], padded[2:3, MAXLAG:], spare])  0.81 us

profile of v1, /device:TPU:13, one launch (start us, length us, event | category | flops | bytes accessed | tf_op | source)
XLA Modules:
  0.0 36.2 jit_solution(6914725900724532521)
XLA Ops:
  0.6 0.0 copy-start.2
  0.6 0.6 %copy-done.2 = s32[2]{0:T(128)S(1)} copy-done((s32[2]{0:T(128)S(1)}, s32[2]{0:T(128)}, u32[]{:S(2)}) %copy-start.2) | copy-done | bytes 32
  1.4 0.0 copy-start.3
  1.4 0.6 %copy-done.3 = s32[1,32]{1,0:T(1,128)S(1)} copy-done((s32[1,32]{1,0:T(1,128)S(1)}, s32[1,32]{1,0:T(1,128)}, u32[]{:S(2)}) %copy-start.3) | copy-done | bytes 152
  2.0 0.7 %subtract_bitcast_fusion = (s32[32]{0:T(128)S(1)}, s32[32]{0:T(128)S(1)}) fusion(s32[8,32]{1,0:T(8,128)} %param.11, s32[]{:T(128)S(6)} %select_n.21, s32[]{:T(128)S(6)} %mul.7, s32[1,32]{1,0:T(1,128)S(1)} %copy-done.3, s32[]{:T(128)S(6)} %mul.6), kind=kLoop, calls=%fused_computation.13 | loop fusion | flops 64 | bytes 524 | tf_op jit(solution)/shard_map/sub | solution.py:195
  2.7 0.1 select_reduce_fusion.2
  2.8 0.1 select_reduce_fusion.3
  3.0 0.1 pad.8.clone
  3.0 0.2 select_reduce_fusion
  3.2 0.0 copy-start.1
  3.2 0.6 %concatenate.6.idx = s32[150]{0:T(256)} concatenate(s32[32]{0:T(128)S(1)} %get-tuple-element.5, s32[32]{0:T(128)S(1)} %get-tuple-element.4, s32[32]{0:T(128)S(1)} %get-tuple-element.3, s32[32]{0:T(128)S(1)} %get-tuple-element.2, s32[4]{0:T(128)S(1)} %select_reduce_fusion.3, s32[16]{0:T(128)S(1)} %select_reduce_fusion.2, s32[2]{0:T(128)S(1)} %copy-done.2), dimensions={0} | concatenate | bytes 1200 | tf_op jit(solution)/shard_map/concatenate | solution.py:208
  3.9 0.0 copy-done.1
  3.9 0.1 pad_slice_fusion
  4.0 0.1 maximum_maximum_fusion
  4.1 0.7 %copy.12 = f32[8,128]{0,1:T(8,128)} copy(f32[8,128]{1,0:T(8,128)S(1)} %maximum_maximum_fusion) | data formatting | bytes 8192 | tf_op jit(solution)/shard_map/concatenate | solution.py:212
  4.8 29.1 %shard_map.86 = (f32[64,512]{1,0:T(8,128)}, f32[16,2048]{1,0:T(8,128)}) custom-call(s32[150]{0:T(256)} %concatenate.6.idx, f32[128,8]{1,0:T(8,128)} %bitcast.9, bf16[16,2048]{1,0:T(8,128)(2,1)} %field.1, bf16[128,512]{1,0:T(8,128)(2,1)} %cot.1, bf16[32,128,128]{2,1,0:T(8,128)(2,1)} %bitcast.8), custom_call_target="tpu_custom_call" | custom-call | flops 268435456 | bytes 2097152 | tf_op jit(solution)/shard_map/pallas_call | solution.py:218
  34.0 0.0 copy-start
  34.0 1.6 %copy.15 = f32[64,512]{1,0:T(8,128)} copy(f32[64,512]{1,0:T(8,128)} %get-tuple-element.10) | data formatting | bytes 262144
  35.6 0.0 copy-done
  35.6 0.7 %copy.16 = f32[16,2048]{1,0:T(8,128)} copy(f32[16,2048]{1,0:T(8,128)S(1)} %copy-done) | data formatting | bytes 262144
  (3 shorter events, 0.0 us)
Async XLA Ops:
  0.6 0.7 %copy-start.2 = (s32[2]{0:T(128)S(1)}, s32[2]{0:T(128)}, u32[]{:S(2)}) copy-start(s32[2]{0:T(128)} %param.12) | copy-start | bytes 28
  1.4 0.7 %copy-start.3 = (s32[1,32]{1,0:T(1,128)S(1)}, s32[1,32]{1,0:T(1,128)}, u32[]{:S(2)}) copy-start(s32[1,32]{1,0:T(1,128)} %param.10) | copy-start | bytes 388
  3.2 0.7 %copy-start.1 = (f32[3,128]{1,0:T(4,128)S(1)}, f32[3,128]{1,0:T(4,128)}, u32[]{:S(2)}) copy-start(f32[3,128]{1,0:T(4,128)} %param.13) | copy-start | bytes 4612
  34.0 1.6 %copy-start = (f32[16,2048]{1,0:T(8,128)S(1)}, f32[16,2048]{1,0:T(8,128)}, u32[]{:S(2)}) copy-start(f32[16,2048]{1,0:T(8,128)} %get-tuple-element.11) | copy-start | bytes 393220

commit v2 on v1

--- a/solution.py
+++ b/solution.py
@@ -11,6 +11,7 @@
 RBD = 4
 TD = 16
 MAXLAG = 24
+PAIR = 2
 F32 = jnp.float32
 BF16 = jnp.bfloat16
 MESH = pl.DeviceIdType.MESH
@@ -39,15 +40,21 @@
     mats_v,
     adj_in,
     sums,
+    adj_part,
     adj_send,
     adj_recv,
+    line_send,
+    line_recv,
     part,
     part_recv,
     local_sem,
     fs_sem,
     fr_sem,
+    fp_sem,
     as_sem,
     ar_sem,
+    ls_sem,
+    lr_sem,
     ps_sem,
     pr_sem,
 ):
@@ -69,23 +76,29 @@
     load_own = pltpu.make_async_copy(field, field_v, local_sem.at[2])
     load_own.start()
 
+    nz = n // PAIR
+    mz, my = me // PAIR, lax.rem(me, PAIR)
+    peer = mz * PAIR + 1 - my
+
+    def on_line(z):
+        return lax.rem(mz + z + nz, nz) * PAIR + my
+
     barrier = pltpu.get_barrier_semaphore()
-    for i in range(1, n):
-        pl.semaphore_signal(
-            barrier, inc=1, device_id={"srow": lax.rem(me + i, n)}, device_id_type=MESH
-        )
+    for i in range(1, nz):
+        pl.semaphore_signal(barrier, inc=1, device_id={"srow": on_line(i)}, device_id_type=MESH)
+    pl.semaphore_signal(barrier, inc=1, device_id={"srow": peer}, device_id_type=MESH)
     pl.semaphore_signal(barrier, inc=1, device_id={"scol": 1 - mc}, device_id_type=MESH)
     load_own.wait()
     for b in range(ncb):
         block = field_v[:, b * BS : (b + 1) * BS]
         field_send[b] = block
         field_all[b, my_rows, :] = block
-    pl.semaphore_wait(barrier, n)
+    pl.semaphore_wait(barrier, nz + 1)
 
     def rows_of(r):
         return pl.ds(pl.multiple_of(r * TD, TD), TD)
 
-    def field_copy(dst, src):
+    def line_copy(dst, src):
         return pltpu.make_async_remote_copy(
             src_ref=field_send,
             dst_ref=field_all.at[:, rows_of(src), :],
@@ -95,18 +108,39 @@
             device_id_type=MESH,
         )
 
-    def adj_copy(dst, src):
+    def peer_copy(src):
         return pltpu.make_async_remote_copy(
-            src_ref=adj_send.at[rows_of(dst), :],
-            dst_ref=adj_recv.at[rows_of(src), :],
-            send_sem=as_sem.at[dst],
-            recv_sem=ar_sem.at[src],
+            src_ref=field_all.at[:, rows_of(src), :],
+            dst_ref=field_all.at[:, rows_of(src), :],
+            send_sem=fp_sem.at[src // PAIR],
+            recv_sem=fr_sem.at[src],
+            device_id={"srow": peer},
+            device_id_type=MESH,
+        )
+
+    def adj_peer_copy(z):
+        return pltpu.make_async_remote_copy(
+            src_ref=adj_send.at[rows_of(z), :],
+            dst_ref=adj_recv.at[rows_of(z), :],
+            send_sem=as_sem.at[z],
+            recv_sem=ar_sem.at[z],
+            device_id={"srow": peer},
+            device_id_type=MESH,
+        )
+
+    def adj_line_copy(dst, src):
+        return pltpu.make_async_remote_copy(
+            src_ref=line_send.at[rows_of(dst // PAIR), :],
+            dst_ref=line_recv.at[rows_of(src // PAIR), :],
+            send_sem=ls_sem.at[dst // PAIR],
+            recv_sem=lr_sem.at[src // PAIR],
             device_id={"srow": dst},
             device_id_type=MESH,
         )
 
-    for i in range(1, n):
-        field_copy(lax.rem(me + i, n), me).start()
+    for i in range(1, nz):
+        line_copy(on_line(i), me).start()
+    peer_copy(me).start()
 
     load_cot.wait()
     spread = coef[...]
@@ -129,14 +163,25 @@
         sums[k + 1] = sums[idx[o_pcol + k]] + product
         return carry
 
-    lax.fori_loop(0, tiles, adj_step, 0, unroll=4)
+    lax.fori_loop(0, tiles // 2, adj_step, 0, unroll=4)
+    line_copy(me, on_line(-1)).wait_recv()
+    peer_copy(on_line(-1)).start()
+    lax.fori_loop(tiles // 2, tiles, adj_step, 0, unroll=4)
     for b in range(ncb):
-        adj_send[:, b * BS : (b + 1) * BS] = sums[idx[o_lcol + b]].astype(BF16)
-    for i in range(1, n):
-        adj_copy(lax.rem(me + i, n), me).start()
-
-    for i in range(1, n):
-        field_copy(me, lax.rem(me + n - i, n)).wait_recv()
+        block = sums[idx[o_lcol + b]].reshape(nz, PAIR, TD, BS)
+        at = slice(b * BS, (b + 1) * BS)
+        mine = jnp.where(my == 0, block[:, 0], block[:, 1])
+        other = jnp.where(my == 0, block[:, 1], block[:, 0])
+        adj_part[:, at] = mine.reshape(half, BS)
+        adj_send[:, at] = other.reshape(half, BS).astype(BF16)
+    for i in range(2, nz):
+        line_copy(me, on_line(-i)).wait_recv()
+        peer_copy(on_line(-i)).start()
+    for i in range(1, nz + 1):
+        adj_peer_copy(lax.rem(mz + i, nz)).start()
+
+    for i in range(nz):
+        peer_copy(lax.rem(mz + nz - i, nz) * PAIR + 1 - my).wait_recv()
 
     def fwd_step(k, carry):
         product = lax.dot_general(
@@ -158,6 +203,14 @@
         device_id_type=MESH,
     )
     exchange.start()
+
+    for i in range(1, nz):
+        z = lax.rem(mz + i, nz)
+        adj_peer_copy(z).wait_recv()
+        total = adj_part[rows_of(z), :] + adj_recv[rows_of(z), :].astype(F32)
+        line_send[rows_of(z), :] = total.astype(BF16)
+        adj_line_copy(on_line(i), me).start()
+
     exchange.wait_recv()
     own = part[pl.ds(pl.multiple_of(mc * half, 8), ext), :]
     value = (own + part_recv[...]).astype(BF16)
@@ -170,17 +223,21 @@
         spread[:, 0:1] * value[MAXLAG:] + spread[:, 1:2] * delayed + spread[:, 2:3] * value[:half]
     )
 
-    adj_out[...] = adj_send[my_rows, :].astype(F32)
-    for i in range(1, n):
-        src = lax.rem(me + n - i, n)
-        adj_copy(me, src).wait_recv()
-        adj_out[...] += adj_recv[rows_of(src), :].astype(F32)
+    adj_peer_copy(mz).wait_recv()
+    total = adj_part[rows_of(mz), :] + adj_recv[rows_of(mz), :].astype(F32)
+    for i in range(1, nz):
+        src = on_line(-i)
+        adj_line_copy(me, src).wait_recv()
+        total += line_recv[rows_of(src // PAIR), :].astype(F32)
+    adj_out[...] = total
 
     exchange.wait_send()
-    for i in range(1, n):
-        dst = lax.rem(me + i, n)
-        field_copy(dst, me).wait_send()
-        adj_copy(dst, me).wait_send()
+    for i in range(1, nz):
+        line_copy(on_line(i), me).wait_send()
+        adj_line_copy(on_line(i), me).wait_send()
+    for i in range(nz):
+        peer_copy(on_line(-i)).wait_send()
+        adj_peer_copy(lax.rem(mz + i, nz)).wait_send()
 
 
 def body(field_in, cotangent, tile_vals, tile_rows, tile_cols, lag_steps, ar_coef):
@@ -214,6 +271,7 @@
     anyspace = pl.BlockSpec(memory_space=pl.ANY)
     vmem = pl.BlockSpec(memory_space=pltpu.VMEM)
     half = hours // 2
+    nz = n // PAIR
     wide = RBD * BS
     return pl.pallas_call(
         functools.partial(kernel, n, tiles, ncb),
@@ -231,15 +289,21 @@
             pltpu.VMEM((tiles, BS, BS), BF16),
             pltpu.VMEM((RBD, hours, BS), BF16),
             pltpu.VMEM((tiles + 1, hours, BS), F32),
-            pltpu.VMEM((hours, cols), BF16),
-            pltpu.VMEM((hours, cols), BF16),
+            pltpu.VMEM((half, cols), F32),
+            pltpu.VMEM((half, cols), BF16),
+            pltpu.VMEM((half, cols), BF16),
+            pltpu.VMEM((half, cols), BF16),
+            pltpu.VMEM((half, cols), BF16),
             pltpu.VMEM((hours + MAXLAG, wide), F32),
             pltpu.VMEM((half + MAXLAG, wide), F32),
             pltpu.SemaphoreType.DMA((3,)),
             pltpu.SemaphoreType.DMA((n,)),
             pltpu.SemaphoreType.DMA((n,)),
-            pltpu.SemaphoreType.DMA((n,)),
-            pltpu.SemaphoreType.DMA((n,)),
+            pltpu.SemaphoreType.DMA((nz,)),
+            pltpu.SemaphoreType.DMA((nz,)),
+            pltpu.SemaphoreType.DMA((nz,)),
+            pltpu.SemaphoreType.DMA((nz,)),
+            pltpu.SemaphoreType.DMA((nz,)),
             pltpu.SemaphoreType.DMA,
             pltpu.SemaphoreType.DMA,
         ],

time: 36.5 us -> 33.1 us (0.907)
  the two profiles are of different devices: /device:TPU:13 before, /device:TPU:0 now
where the time goes in v2:
time: 33.1 us; the launch traced here: 32.9 us
  Pallas kernels  25.8 us (78%)
  local copies, waits for them, and re-layouts  5.09 us (15%)
  other arithmetic  1.19 us (4%)
  between operations  0.8 us (2%)
    pallas_call x1, Pallas kernels, body(): pl.pallas_call(functools.partial(kernel, n, tiles, ncb), out_shape=(jax.S...  25.8 us
    unnamed x10, local copies, waits for them, and re-layouts  3.55 us
    concatenate x2, local copies, waits for them, and re-layouts, body(): jnp.concatenate([ar_coef, ahead[None], padded[2:3, MAXLAG:], spare])  0.81 us
    sub x1, other arithmetic, body(): lax.dynamic_slice_in_dim(tile_cols, row_index, 1, 0)[0] - col_index * ncb  0.69 us

profile of v2, /device:TPU:0, one launch (start us, length us, event | category | flops | bytes accessed | tf_op | source)
XLA Modules:
  0.0 32.9 jit_solution(8373736427102505364)
XLA Ops:
  0.6 0.0 copy-start.2
  0.6 0.6 %copy-done.2 = s32[2]{0:T(128)S(1)} copy-done((s32[2]{0:T(128)S(1)}, s32[2]{0:T(128)}, u32[]{:S(2)}) %copy-start.2) | copy-done | bytes 32
  1.4 0.0 copy-start.3
  1.4 0.6 %copy-done.3 = s32[1,32]{1,0:T(1,128)S(1)} copy-done((s32[1,32]{1,0:T(1,128)S(1)}, s32[1,32]{1,0:T(1,128)}, u32[]{:S(2)}) %copy-start.3) | copy-done | bytes 152
  2.0 0.7 %subtract_bitcast_fusion = (s32[32]{0:T(128)S(1)}, s32[32]{0:T(128)S(1)}) fusion(s32[8,32]{1,0:T(8,128)} %param.11, s32[]{:T(128)S(6)} %select_n.21, s32[]{:T(128)S(6)} %mul.7, s32[1,32]{1,0:T(1,128)S(1)} %copy-done.3, s32[]{:T(128)S(6)} %mul.6), kind=kLoop, calls=%fused_computation.13 | loop fusion | flops 64 | bytes 524 | tf_op jit(solution)/shard_map/sub | solution.py:252
  2.7 0.1 select_reduce_fusion.2
  2.8 0.1 select_reduce_fusion.3
  3.0 0.1 pad.8.clone
  3.0 0.2 select_reduce_fusion
  3.2 0.0 copy-start.1
  3.2 0.6 %concatenate.6.idx = s32[150]{0:T(256)} concatenate(s32[32]{0:T(128)S(1)} %get-tuple-element.5, s32[32]{0:T(128)S(1)} %get-tuple-element.4, s32[32]{0:T(128)S(1)} %get-tuple-element.3, s32[32]{0:T(128)S(1)} %get-tuple-element.2, s32[4]{0:T(128)S(1)} %select_reduce_fusion.3, s32[16]{0:T(128)S(1)} %select_reduce_fusion.2, s32[2]{0:T(128)S(1)} %copy-done.2), dimensions={0} | concatenate | bytes 1200 | tf_op jit(solution)/shard_map/concatenate | solution.py:265
  3.9 0.0 copy-done.1
  3.9 0.1 pad_slice_fusion
  4.0 0.1 maximum_maximum_fusion
  4.1 0.7 %copy.12 = f32[8,128]{0,1:T(8,128)} copy(f32[8,128]{1,0:T(8,128)S(1)} %maximum_maximum_fusion) | data formatting | bytes 8192 | tf_op jit(solution)/shard_map/concatenate | solution.py:269
  4.8 25.8 %shard_map.86 = (f32[64,512]{1,0:T(8,128)}, f32[16,2048]{1,0:T(8,128)}) custom-call(s32[150]{0:T(256)} %concatenate.6.idx, f32[128,8]{1,0:T(8,128)} %bitcast.9, bf16[16,2048]{1,0:T(8,128)(2,1)} %field.1, bf16[128,512]{1,0:T(8,128)(2,1)} %cot.1, bf16[32,128,128]{2,1,0:T(8,128)(2,1)} %bitcast.8), custom_call_target="tpu_custom_call" | custom-call | flops 268435456 | bytes 2097152 | tf_op jit(solution)/shard_map/pallas_call | solution.py:276
  30.6 0.0 copy-start
  30.6 1.6 %copy.15 = f32[64,512]{1,0:T(8,128)} copy(f32[64,512]{1,0:T(8,128)} %get-tuple-element.10) | data formatting | bytes 262144
  32.2 0.0 copy-done
  32.2 0.7 %copy.16 = f32[16,2048]{1,0:T(8,128)} copy(f32[16,2048]{1,0:T(8,128)S(1)} %copy-done) | data formatting | bytes 262144
  (3 shorter events, 0.0 us)
Async XLA Ops:
  0.6 0.7 %copy-start.2 = (s32[2]{0:T(128)S(1)}, s32[2]{0:T(128)}, u32[]{:S(2)}) copy-start(s32[2]{0:T(128)} %param.12) | copy-start | bytes 28
  1.4 0.7 %copy-start.3 = (s32[1,32]{1,0:T(1,128)S(1)}, s32[1,32]{1,0:T(1,128)}, u32[]{:S(2)}) copy-start(s32[1,32]{1,0:T(1,128)} %param.10) | copy-start | bytes 388
  3.2 0.7 %copy-start.1 = (f32[3,128]{1,0:T(4,128)S(1)}, f32[3,128]{1,0:T(4,128)}, u32[]{:S(2)}) copy-start(f32[3,128]{1,0:T(4,128)} %param.13) | copy-start | bytes 4612
  30.6 1.6 %copy-start = (f32[16,2048]{1,0:T(8,128)S(1)}, f32[16,2048]{1,0:T(8,128)}, u32[]{:S(2)}) copy-start(f32[16,2048]{1,0:T(8,128)} %get-tuple-element.11) | copy-start | bytes 393220

commit v3 on v2

--- a/solution.py
+++ b/solution.py
@@ -163,10 +163,7 @@
         sums[k + 1] = sums[idx[o_pcol + k]] + product
         return carry
 
-    lax.fori_loop(0, tiles // 2, adj_step, 0, unroll=4)
-    line_copy(me, on_line(-1)).wait_recv()
-    peer_copy(on_line(-1)).start()
-    lax.fori_loop(tiles // 2, tiles, adj_step, 0, unroll=4)
+    lax.fori_loop(0, tiles, adj_step, 0, unroll=4)
     for b in range(ncb):
         block = sums[idx[o_lcol + b]].reshape(nz, PAIR, TD, BS)
         at = slice(b * BS, (b + 1) * BS)
@@ -174,11 +171,18 @@
         other = jnp.where(my == 0, block[:, 1], block[:, 0])
         adj_part[:, at] = mine.reshape(half, BS)
         adj_send[:, at] = other.reshape(half, BS).astype(BF16)
-    for i in range(2, nz):
+    for i in range(1, nz + 1):
+        adj_peer_copy(lax.rem(mz + i, nz)).start()
+    for i in range(1, nz):
         line_copy(me, on_line(-i)).wait_recv()
         peer_copy(on_line(-i)).start()
-    for i in range(1, nz + 1):
-        adj_peer_copy(lax.rem(mz + i, nz)).start()
+
+    for i in range(1, nz):
+        z = lax.rem(mz + i, nz)
+        adj_peer_copy(z).wait_recv()
+        total = adj_part[rows_of(z), :] + adj_recv[rows_of(z), :].astype(F32)
+        line_send[rows_of(z), :] = total.astype(BF16)
+        adj_line_copy(on_line(i), me).start()
 
     for i in range(nz):
         peer_copy(lax.rem(mz + nz - i, nz) * PAIR + 1 - my).wait_recv()
@@ -203,14 +207,6 @@
         device_id_type=MESH,
     )
     exchange.start()
-
-    for i in range(1, nz):
-        z = lax.rem(mz + i, nz)
-        adj_peer_copy(z).wait_recv()
-        total = adj_part[rows_of(z), :] + adj_recv[rows_of(z), :].astype(F32)
-        line_send[rows_of(z), :] = total.astype(BF16)
-        adj_line_copy(on_line(i), me).start()
-
     exchange.wait_recv()
     own = part[pl.ds(pl.multiple_of(mc * half, 8), ext), :]
     value = (own + part_recv[...]).astype(BF16)

time: 33.1 us -> 30.9 us (0.934)
  Pallas kernels: 25.8 us -> 23.4 us
    pallas_call x1, Pallas kernels: 25.8 us -> 23.4 us  [body(): pl.pallas_call(functools.partial(kernel, n, tiles, ncb), out_shape=(jax.S...]
where the time goes in v3:
time: 30.9 us; the launch traced here: 30.5 us
  Pallas kernels  23.4 us (76%)
  local copies, waits for them, and re-layouts  5.09 us (16%)
  other arithmetic  1.19 us (4%)
  between operations  0.8 us (3%)
    pallas_call x1, Pallas kernels, body(): pl.pallas_call(functools.partial(kernel, n, tiles, ncb), out_shape=(jax.S...  23.4 us
    unnamed x10, local copies, waits for them, and re-layouts  3.55 us
    concatenate x2, local copies, waits for them, and re-layouts, body(): jnp.concatenate([ar_coef, ahead[None], padded[2:3, MAXLAG:], spare])  0.81 us
    sub x1, other arithmetic, body(): lax.dynamic_slice_in_dim(tile_cols, row_index, 1, 0)[0] - col_index * ncb  0.69 us
    concatenate x1, local copies, waits for them, and re-layouts, body(): idx = jnp.concatenate([rows, own_cols, prow, pcol, lrow, lcol, lag_steps])  0.65 us

profile of v3, /device:TPU:0, one launch (start us, length us, event | category | flops | bytes accessed | tf_op | source)
XLA Modules:
  0.0 30.5 jit_solution(13274703056073278532)
XLA Ops:
  0.6 0.0 copy-start.2
  0.6 0.6 %copy-done.2 = s32[2]{0:T(128)S(1)} copy-done((s32[2]{0:T(128)S(1)}, s32[2]{0:T(128)}, u32[]{:S(2)}) %copy-start.2) | copy-done | bytes 32
  1.4 0.0 copy-start.3
  1.4 0.6 %copy-done.3 = s32[1,32]{1,0:T(1,128)S(1)} copy-done((s32[1,32]{1,0:T(1,128)S(1)}, s32[1,32]{1,0:T(1,128)}, u32[]{:S(2)}) %copy-start.3) | copy-done | bytes 152
  2.0 0.7 %subtract_bitcast_fusion = (s32[32]{0:T(128)S(1)}, s32[32]{0:T(128)S(1)}) fusion(s32[8,32]{1,0:T(8,128)} %param.11, s32[]{:T(128)S(6)} %select_n.21, s32[]{:T(128)S(6)} %mul.7, s32[1,32]{1,0:T(1,128)S(1)} %copy-done.3, s32[]{:T(128)S(6)} %mul.6), kind=kLoop, calls=%fused_computation.13 | loop fusion | flops 64 | bytes 524 | tf_op jit(solution)/shard_map/sub | solution.py:248
  2.7 0.1 select_reduce_fusion.2
  2.8 0.1 select_reduce_fusion.3
  3.0 0.1 pad.8.clone
  3.0 0.2 select_reduce_fusion
  3.2 0.0 copy-start.1
  3.2 0.6 %concatenate.6.idx = s32[150]{0:T(256)} concatenate(s32[32]{0:T(128)S(1)} %get-tuple-element.5, s32[32]{0:T(128)S(1)} %get-tuple-element.4, s32[32]{0:T(128)S(1)} %get-tuple-element.3, s32[32]{0:T(128)S(1)} %get-tuple-element.2, s32[4]{0:T(128)S(1)} %select_reduce_fusion.3, s32[16]{0:T(128)S(1)} %select_reduce_fusion.2, s32[2]{0:T(128)S(1)} %copy-done.2), dimensions={0} | concatenate | bytes 1200 | tf_op jit(solution)/shard_map/concatenate | solution.py:261
  3.9 0.0 copy-done.1
  3.9 0.1 pad_slice_fusion
  4.0 0.1 maximum_maximum_fusion
  4.1 0.7 %copy.12 = f32[8,128]{0,1:T(8,128)} copy(f32[8,128]{1,0:T(8,128)S(1)} %maximum_maximum_fusion) | data formatting | bytes 8192 | tf_op jit(solution)/shard_map/concatenate | solution.py:265
  4.8 23.4 %shard_map.86 = (f32[64,512]{1,0:T(8,128)}, f32[16,2048]{1,0:T(8,128)}) custom-call(s32[150]{0:T(256)} %concatenate.6.idx, f32[128,8]{1,0:T(8,128)} %bitcast.9, bf16[16,2048]{1,0:T(8,128)(2,1)} %field.1, bf16[128,512]{1,0:T(8,128)(2,1)} %cot.1, bf16[32,128,128]{2,1,0:T(8,128)(2,1)} %bitcast.8), custom_call_target="tpu_custom_call" | custom-call | flops 268435456 | bytes 2097152 | tf_op jit(solution)/shard_map/pallas_call | solution.py:272
  28.2 0.0 copy-start
  28.2 1.6 %copy.15 = f32[64,512]{1,0:T(8,128)} copy(f32[64,512]{1,0:T(8,128)} %get-tuple-element.10) | data formatting | bytes 262144
  29.8 0.0 copy-done
  29.8 0.7 %copy.16 = f32[16,2048]{1,0:T(8,128)} copy(f32[16,2048]{1,0:T(8,128)S(1)} %copy-done) | data formatting | bytes 262144
  (3 shorter events, 0.0 us)
Async XLA Ops:
  0.6 0.7 %copy-start.2 = (s32[2]{0:T(128)S(1)}, s32[2]{0:T(128)}, u32[]{:S(2)}) copy-start(s32[2]{0:T(128)} %param.12) | copy-start | bytes 28
  1.4 0.7 %copy-start.3 = (s32[1,32]{1,0:T(1,128)S(1)}, s32[1,32]{1,0:T(1,128)}, u32[]{:S(2)}) copy-start(s32[1,32]{1,0:T(1,128)} %param.10) | copy-start | bytes 388
  3.2 0.7 %copy-start.1 = (f32[3,128]{1,0:T(4,128)S(1)}, f32[3,128]{1,0:T(4,128)}, u32[]{:S(2)}) copy-start(f32[3,128]{1,0:T(4,128)} %param.13) | copy-start | bytes 4612
  28.2 1.6 %copy-start = (f32[16,2048]{1,0:T(8,128)S(1)}, f32[16,2048]{1,0:T(8,128)}, u32[]{:S(2)}) copy-start(f32[16,2048]{1,0:T(8,128)} %get-tuple-element.11) | copy-start | bytes 393220

commit v4 on v3

--- a/solution.py
+++ b/solution.py
@@ -17,6 +17,11 @@
 MESH = pl.DeviceIdType.MESH
 
 
+def iotas(rows, cols):
+    shape = (rows, cols)
+    return lax.broadcasted_iota(jnp.int32, shape, 0), lax.broadcasted_iota(jnp.int32, shape, 1)
+
+
 def shift_matrix(rows, cols, lag):
     at = lax.broadcasted_iota(jnp.int32, (rows, cols), 0) + lag
     return (lax.broadcasted_iota(jnp.int32, (rows, cols), 1) == at).astype(F32).astype(BF16)
@@ -26,13 +31,22 @@
     n,
     tiles,
     ncb,
-    idx,
-    coef,
     field,
     cot,
     mats,
+    tile_rows,
+    tile_cols,
+    lags,
+    ar_coef,
     fwd_out,
     adj_out,
+    rows_v,
+    cols_v,
+    lags_s,
+    coef_v,
+    coef,
+    idx_v,
+    idx,
     field_all,
     field_v,
     field_send,
@@ -63,18 +77,21 @@
     ext = half + MAXLAG
     me = lax.axis_index("srow")
     mc = lax.axis_index("scol")
-    o_row, o_col, o_prow, o_pcol = 0, tiles, 2 * tiles, 3 * tiles
-    o_lrow = 4 * tiles
-    o_lcol = o_lrow + RBD
-    o_lag = o_lcol + ncb
-
+    small = [
+        pltpu.make_async_copy(src, dst, local_sem.at[3 + i])
+        for i, (src, dst) in enumerate(
+            ((tile_rows, rows_v), (tile_cols, cols_v), (lags, lags_s), (ar_coef, coef_v))
+        )
+    ]
     load_cot = pltpu.make_async_copy(cot, cot_v, local_sem.at[0])
     load_mats = pltpu.make_async_copy(mats, mats_v, local_sem.at[1])
-    load_cot.start()
-    load_mats.start()
     my_rows = pl.ds(pl.multiple_of(me * TD, TD), TD)
     load_own = pltpu.make_async_copy(field, field_v, local_sem.at[2])
     load_own.start()
+    for copy in small:
+        copy.start()
+    load_cot.start()
+    load_mats.start()
 
     nz = n // PAIR
     mz, my = me // PAIR, lax.rem(me, PAIR)
@@ -93,6 +110,32 @@
         block = field_v[:, b * BS : (b + 1) * BS]
         field_send[b] = block
         field_all[b, my_rows, :] = block
+    for copy in small:
+        copy.wait()
+    lag1 = lags_s[0]
+    at_row, at_col = iotas(n, tiles)
+    own_cols = jnp.sum(jnp.where(at_row == me, cols_v[...], 0), 0, keepdims=True)
+    table = [
+        jnp.clip(rows_v[...] - me * RBD, 0, RBD - 1),
+        jnp.clip(own_cols - mc * ncb, 0, ncb - 1),
+    ]
+    at_row, at_col = iotas(tiles, tiles)
+    for ids in (table[0], table[1]):
+        column = jnp.sum(jnp.where(at_row == at_col, ids, 0), 1, keepdims=True)
+        same = (column == ids) & (at_row < at_col)
+        table.append(jnp.max(jnp.where(same, at_row + 1, 0), 0, keepdims=True))
+        block_row, block = iotas(tiles, BS)
+        table.append(jnp.max(jnp.where(column == block, block_row + 1, 0), 0, keepdims=True))
+    idx_v[...] = jnp.zeros_like(idx_v)
+    for i, row in enumerate(table):
+        idx_v[i : i + 1, 0 : row.shape[1]] = row
+    place = pltpu.make_async_copy(idx_v, idx, local_sem.at[7])
+    place.start()
+    at_row, at_col = iotas(hours, hours)
+    terms = ((0, 0), (1, 0), (2, 0), (1, lag1), (2, MAXLAG))
+    for i, (term, lag) in enumerate(terms):
+        line = jnp.where(at_col == at_row + lag, coef_v[term : term + 1, :], 0.0)
+        coef[:, i : i + 1] = jnp.sum(line, 1, keepdims=True)
     pl.semaphore_wait(barrier, nz + 1)
 
     def rows_of(r):
@@ -144,7 +187,6 @@
 
     load_cot.wait()
     spread = coef[...]
-    lag1 = idx[o_lag]
     early = cot_v[...]
     wide = early.astype(F32)
     later = jnp.dot(shift_matrix(hours, hours, lag1), early, preferred_element_type=F32)
@@ -155,17 +197,18 @@
     for r in range(RBD):
         adj_in[r] = adjoint[:, r * BS : (r + 1) * BS]
 
+    place.wait()
     load_mats.wait()
     sums[0] = jnp.zeros((hours, BS), F32)
 
     def adj_step(k, carry):
-        product = jnp.dot(adj_in[idx[o_row + k]], mats_v[k], preferred_element_type=F32)
-        sums[k + 1] = sums[idx[o_pcol + k]] + product
+        product = jnp.dot(adj_in[idx[0, k]], mats_v[k], preferred_element_type=F32)
+        sums[k + 1] = sums[idx[4, k]] + product
         return carry
 
     lax.fori_loop(0, tiles, adj_step, 0, unroll=4)
     for b in range(ncb):
-        block = sums[idx[o_lcol + b]].reshape(nz, PAIR, TD, BS)
+        block = sums[idx[5, b]].reshape(nz, PAIR, TD, BS)
         at = slice(b * BS, (b + 1) * BS)
         mine = jnp.where(my == 0, block[:, 0], block[:, 1])
         other = jnp.where(my == 0, block[:, 1], block[:, 0])
@@ -189,15 +232,15 @@
 
     def fwd_step(k, carry):
         product = lax.dot_general(
-            field_all[idx[o_col + k]], mats_v[k], (((1,), (1,)), ((), ())), preferred_element_type=F32
-        )
-        sums[k + 1] = sums[idx[o_prow + k]] + product
+            field_all[idx[1, k]], mats_v[k], (((1,), (1,)), ((), ())), preferred_element_type=F32
+        )
+        sums[k + 1] = sums[idx[2, k]] + product
         return carry
 
     lax.fori_loop(0, tiles, fwd_step, 0, unroll=4)
     part[pl.ds(0, MAXLAG), :] = jnp.zeros((MAXLAG, RBD * BS), F32)
     for r in range(RBD):
-        part[pl.ds(MAXLAG, hours), r * BS : (r + 1) * BS] = sums[idx[o_lrow + r]]
+        part[pl.ds(MAXLAG, hours), r * BS : (r + 1) * BS] = sums[idx[3, r]]
     exchange = pltpu.make_async_remote_copy(
         src_ref=part.at[pl.ds(pl.multiple_of((1 - mc) * half, 8), ext), :],
         dst_ref=part_recv,
@@ -238,32 +281,10 @@
 
 def body(field_in, cotangent, tile_vals, tile_rows, tile_cols, lag_steps, ar_coef):
     n = lax.axis_size("srow")
-    row_index = lax.axis_index("srow")
-    col_index = lax.axis_index("scol")
     tiles = tile_vals.shape[1]
     cols = field_in.shape[1]
     ncb = cols // BS
     hours = n * TD
-    rows = tile_rows[0] - row_index * RBD
-    own_cols = lax.dynamic_slice_in_dim(tile_cols, row_index, 1, 0)[0] - col_index * ncb
-    place = jnp.arange(tiles, dtype=jnp.int32)
-    earlier = place[None, :] < place[:, None]
-
-    def chain(ids, blocks):
-        same = (ids[:, None] == ids[None, :]) & earlier
-        prev = jnp.max(jnp.where(same, place[None, :] + 1, 0), axis=1)
-        which = jnp.arange(blocks, dtype=jnp.int32)[:, None] == ids[None, :]
-        last = jnp.max(jnp.where(which, place[None, :] + 1, 0), axis=1)
-        return prev, last
-
-    prow, lrow = chain(rows, RBD)
-    pcol, lcol = chain(own_cols, ncb)
-    idx = jnp.concatenate([rows, own_cols, prow, pcol, lrow, lcol, lag_steps])
-    padded = jnp.pad(ar_coef, ((0, 0), (0, MAXLAG)))
-    ahead = lax.dynamic_slice_in_dim(padded[1], lag_steps[0], hours)
-    spare = jnp.zeros((3, hours), F32)
-    coef = jnp.concatenate([ar_coef, ahead[None], padded[2:3, MAXLAG:], spare]).T
-
     anyspace = pl.BlockSpec(memory_space=pl.ANY)
     vmem = pl.BlockSpec(memory_space=pltpu.VMEM)
     half = hours // 2
@@ -275,9 +296,16 @@
             jax.ShapeDtypeStruct((half, wide), F32),
             jax.ShapeDtypeStruct((TD, cols), F32),
         ),
-        in_specs=[pl.BlockSpec(memory_space=pltpu.SMEM), vmem, anyspace, anyspace, anyspace],
+        in_specs=[anyspace] * 7,
         out_specs=(vmem, vmem),
         scratch_shapes=[
+            pltpu.VMEM((1, tiles), jnp.int32),
+            pltpu.VMEM((n, tiles), jnp.int32),
+            pltpu.SMEM((2,), jnp.int32),
+            pltpu.VMEM((3, hours), F32),
+            pltpu.VMEM((hours, 8), F32),
+            pltpu.VMEM((8, BS), jnp.int32),
+            pltpu.SMEM((8, BS), jnp.int32),
             pltpu.VMEM((ncb, hours, BS), BF16),
             pltpu.VMEM((TD, cols), BF16),
             pltpu.VMEM((ncb, TD, BS), BF16),
@@ -292,7 +320,7 @@
             pltpu.VMEM((half, cols), BF16),
             pltpu.VMEM((hours + MAXLAG, wide), F32),
             pltpu.VMEM((half + MAXLAG, wide), F32),
-            pltpu.SemaphoreType.DMA((3,)),
+            pltpu.SemaphoreType.DMA((8,)),
             pltpu.SemaphoreType.DMA((n,)),
             pltpu.SemaphoreType.DMA((n,)),
             pltpu.SemaphoreType.DMA((nz,)),
@@ -309,7 +337,7 @@
         cost_estimate=pl.CostEstimate(
             flops=4 * tiles * hours * BS * BS, bytes_accessed=2 << 20, transcendentals=0
         ),
-    )(idx, coef, field_in, cotangent, tile_vals[0])
+    )(field_in, cotangent, tile_vals[0], tile_rows, tile_cols, lag_steps, ar_coef)
 
 
 def solution(mesh):

time: 30.9 us -> 25.8 us (0.83)
  local copies, waits for them, and re-layouts: 5.09 us -> 2.26 us
  other arithmetic: 1.19 us -> 0 us
  Pallas kernels: 23.4 us -> 22.6 us
    concatenate x3 -> x0, local copies, waits for them, and re-layouts: 1.46 us -> none  [the longest x2 0.81 us: body(): jnp.concatenate([ar_coef, ahead[None], padded[2:3, MAXLAG:], spare])]
    unnamed x10 -> x4, local copies, waits for them, and re-layouts: 3.55 us -> 2.26 us
    pallas_call x1, Pallas kernels: 23.4 us -> 22.6 us  [body(): pl.pallas_call(functools.partial(kernel, n, tiles, ncb), out_shape=(jax.S...]
    sub x1 -> x0, other arithmetic: 0.69 us -> none  [body(): lax.dynamic_slice_in_dim(tile_cols, row_index, 1, 0)[0] - col_index * ncb]
    reduce_max x3 -> x0, other arithmetic: 0.42 us -> none  [the longest x2 0.24 us: chain(): last = jnp.max(jnp.where(which, place[None, :] + 1, 0), axis=1)]
where the time goes in v4:
time: 25.8 us; the launch traced here: 25.5 us
  Pallas kernels  22.6 us (88%)
  local copies, waits for them, and re-layouts  2.26 us (9%)
  between operations  0.65 us (3%)
    pallas_call x1, Pallas kernels, body(): pl.pallas_call(functools.partial(kernel, n, tiles, ncb), out_shape=(jax.S...  22.6 us
    unnamed x4, local copies, waits for them, and re-layouts  2.26 us

profile of v4, /device:TPU:0, one launch (start us, length us, event | category | flops | bytes accessed | tf_op | source)
XLA Modules:
  0.0 25.5 jit_solution(16331808818301658032)
XLA Ops:
  0.6 22.6 %shard_map.86 = (f32[64,512]{1,0:T(8,128)}, f32[16,2048]{1,0:T(8,128)}) custom-call(bf16[16,2048]{1,0:T(8,128)(2,1)} %field.1, bf16[128,512]{1,0:T(8,128)(2,1)} %cot.1, bf16[32,128,128]{2,1,0:T(8,128)(2,1)} %bitcast.1, s32[1,32]{1,0:T(1,128)} %tile_rows.1, s32[8,32]{1,0:T(8,128)} %tile_cols.1, s32[2]{0:T(128)} %lags.1, f32[3,128]{1,0:T(4,128)} %ar_coef.1), custom_call_target="tpu_custom_call" | custom-call | flops 268435456 | bytes 2097152 | tf_op jit(solution)/shard_map/pallas_call | solution.py:293
  23.3 0.0 copy-start
  23.3 1.6 %copy.11 = f32[64,512]{1,0:T(8,128)} copy(f32[64,512]{1,0:T(8,128)} %get-tuple-element.4) | data formatting | bytes 262144
  24.9 0.0 copy-done
  24.9 0.7 %copy.12 = f32[16,2048]{1,0:T(8,128)} copy(f32[16,2048]{1,0:T(8,128)S(1)} %copy-done) | data formatting | bytes 262144
Async XLA Ops:
  23.3 1.6 %copy-start = (f32[16,2048]{1,0:T(8,128)S(1)}, f32[16,2048]{1,0:T(8,128)}, u32[]{:S(2)}) copy-start(f32[16,2048]{1,0:T(8,128)} %get-tuple-element.5) | copy-start | bytes 393220

commit v5 on v4

--- a/solution.py
+++ b/solution.py
@@ -279,6 +279,15 @@
         adj_peer_copy(lax.rem(mz + i, nz)).wait_send()
 
 
+def hand_over(fwd, adj, fwd_out, adj_out, sem):
+    first = pltpu.make_async_copy(fwd, fwd_out, sem.at[0])
+    second = pltpu.make_async_copy(adj, adj_out, sem.at[1])
+    first.start()
+    second.start()
+    first.wait()
+    second.wait()
+
+
 def body(field_in, cotangent, tile_vals, tile_rows, tile_cols, lag_steps, ar_coef):
     n = lax.axis_size("srow")
     tiles = tile_vals.shape[1]
@@ -290,7 +299,7 @@
     half = hours // 2
     nz = n // PAIR
     wide = RBD * BS
-    return pl.pallas_call(
+    results = pl.pallas_call(
         functools.partial(kernel, n, tiles, ncb),
         out_shape=(
             jax.ShapeDtypeStruct((half, wide), F32),
@@ -338,6 +347,13 @@
             flops=4 * tiles * hours * BS * BS, bytes_accessed=2 << 20, transcendentals=0
         ),
     )(field_in, cotangent, tile_vals[0], tile_rows, tile_cols, lag_steps, ar_coef)
+    return pl.pallas_call(
+        hand_over,
+        out_shape=[jax.ShapeDtypeStruct(value.shape, F32) for value in results],
+        in_specs=[anyspace] * 2,
+        out_specs=[anyspace] * 2,
+        scratch_shapes=[pltpu.SemaphoreType.DMA((2,))],
+    )(*results)
 
 
 def solution(mesh):

time: 25.8 us -> 32.6 us (1.26)
  Pallas kernels: 22.6 us -> 31.7 us
  local copies, waits for them, and re-layouts: 2.26 us -> 0 us
    pallas_call x0 -> x1, Pallas kernels: none -> 9.06 us  [body(): pl.pallas_call(hand_over, out_shape=[jax.ShapeDtypeStruct(value.shape, F3...]
    unnamed x4 -> x0, local copies, waits for them, and re-layouts: 2.26 us -> none
where the time goes in v5:
time: 32.6 us; the launch traced here: 32.3 us
  Pallas kernels  31.7 us (97%)
  between operations  0.64 us (2%)
    pallas_call x1, Pallas kernels, body(): pl.pallas_call(functools.partial(kernel, n, tiles, ncb), out_shape=(jax.S...  22.6 us
    pallas_call x1, Pallas kernels, body(): pl.pallas_call(hand_over, out_shape=[jax.ShapeDtypeStruct(value.shape, F3...  9.06 us

profile of v5, /device:TPU:0, one launch (start us, length us, event | category | flops | bytes accessed | tf_op | source)
XLA Modules:
  0.0 32.3 jit_solution(9648880037101059702)
XLA Ops:
  0.6 22.6 %shard_map.86 = (f32[64,512]{1,0:T(8,128)}, f32[16,2048]{1,0:T(8,128)}) custom-call(bf16[16,2048]{1,0:T(8,128)(2,1)} %field.1, bf16[128,512]{1,0:T(8,128)(2,1)} %cot.1, bf16[32,128,128]{2,1,0:T(8,128)(2,1)} %bitcast.1, s32[1,32]{1,0:T(1,128)} %tile_rows.1, s32[8,32]{1,0:T(8,128)} %tile_cols.1, s32[2]{0:T(128)} %lags.1, f32[3,128]{1,0:T(4,128)} %ar_coef.1), custom_call_target="tpu_custom_call" | custom-call | flops 268435456 | bytes 2097152 | tf_op jit(solution)/shard_map/pallas_call | solution.py:302
  23.3 9.1 %shard_map.87 = (f32[64,512]{1,0:T(8,128)}, f32[16,2048]{1,0:T(8,128)}) custom-call(f32[64,512]{1,0:T(8,128)} %get-tuple-element.4.fwd, f32[16,2048]{1,0:T(8,128)} %get-tuple-element.5.adj), custom_call_target="tpu_custom_call" | custom-call | tf_op jit(solution)/shard_map/pallas_call | solution.py:350

commit v6 on v4

--- a/solution.py
+++ b/solution.py
@@ -49,7 +49,6 @@
     idx,
     field_all,
     field_v,
-    field_send,
     cot_v,
     mats_v,
     adj_in,
@@ -108,7 +107,6 @@
     load_own.wait()
     for b in range(ncb):
         block = field_v[:, b * BS : (b + 1) * BS]
-        field_send[b] = block
         field_all[b, my_rows, :] = block
     for copy in small:
         copy.wait()
@@ -141,13 +139,13 @@
     def rows_of(r):
         return pl.ds(pl.multiple_of(r * TD, TD), TD)
 
-    def line_copy(dst, src):
+    def line_copy(way, src):
         return pltpu.make_async_remote_copy(
-            src_ref=field_send,
+            src_ref=field_all.at[:, rows_of(src), :],
             dst_ref=field_all.at[:, rows_of(src), :],
-            send_sem=fs_sem.at[dst],
+            send_sem=fs_sem.at[(1 + way) // 2 * nz + src // PAIR],
             recv_sem=fr_sem.at[src],
-            device_id={"srow": dst},
+            device_id={"srow": me + way * PAIR},
             device_id_type=MESH,
         )
 
@@ -181,8 +179,28 @@
             device_id_type=MESH,
         )
 
-    for i in range(1, nz):
-        line_copy(on_line(i), me).start()
+    ways = (1, -1)
+
+    def arrival(step, way, act):
+        z = mz - way * step
+        pl.when((z >= 0) & (z < nz))(lambda: act(z * PAIR + my))
+
+    def onward(src, way, act):
+        z = mz + way
+        pl.when((z >= 0) & (z < nz))(lambda: act(line_copy(way, src)))
+
+    def pass_on(step):
+        for way in ways:
+
+            def act(src, way=way):
+                line_copy(way, src).wait_recv()
+                onward(src, way, lambda copy: copy.start())
+                peer_copy(src).start()
+
+            arrival(step, way, act)
+
+    for way in ways:
+        onward(me, way, lambda copy: copy.start())
     peer_copy(me).start()
 
     load_cot.wait()
@@ -206,7 +224,9 @@
         sums[k + 1] = sums[idx[4, k]] + product
         return carry
 
-    lax.fori_loop(0, tiles, adj_step, 0, unroll=4)
+    lax.fori_loop(0, tiles // 2, adj_step, 0, unroll=4)
+    pass_on(1)
+    lax.fori_loop(tiles // 2, tiles, adj_step, 0, unroll=4)
     for b in range(ncb):
         block = sums[idx[5, b]].reshape(nz, PAIR, TD, BS)
         at = slice(b * BS, (b + 1) * BS)
@@ -217,8 +237,8 @@
     for i in range(1, nz + 1):
         adj_peer_copy(lax.rem(mz + i, nz)).start()
     for i in range(1, nz):
-        line_copy(me, on_line(-i)).wait_recv()
-        peer_copy(on_line(-i)).start()
+        if i > 1:
+            pass_on(i)
 
     for i in range(1, nz):
         z = lax.rem(mz + i, nz)
@@ -272,8 +292,15 @@
 
     exchange.wait_send()
     for i in range(1, nz):
-        line_copy(on_line(i), me).wait_send()
         adj_line_copy(on_line(i), me).wait_send()
+    for way in ways:
+        onward(me, way, lambda copy: copy.wait_send())
+        for i in range(1, nz):
+
+            def sent(src, way=way):
+                onward(src, way, lambda copy: copy.wait_send())
+
+            arrival(i, way, sent)
     for i in range(nz):
         peer_copy(on_line(-i)).wait_send()
         adj_peer_copy(lax.rem(mz + i, nz)).wait_send()
@@ -308,7 +335,6 @@
             pltpu.SMEM((8, BS), jnp.int32),
             pltpu.VMEM((ncb, hours, BS), BF16),
             pltpu.VMEM((TD, cols), BF16),
-            pltpu.VMEM((ncb, TD, BS), BF16),
             pltpu.VMEM((hours, wide), BF16),
             pltpu.VMEM((tiles, BS, BS), BF16),
             pltpu.VMEM((RBD, hours, BS), BF16),

time: 25.8 us -> 26.1 us (1.012)
  Pallas kernels: 22.6 us -> 22.9 us
where the time goes in v6:
time: 26.1 us; the launch traced here: 25.8 us
  Pallas kernels  22.9 us (88%)
  local copies, waits for them, and re-layouts  2.26 us (9%)
  between operations  0.65 us (2%)
    pallas_call x1, Pallas kernels, body(): pl.pallas_call(functools.partial(kernel, n, tiles, ncb), out_shape=(jax.S...  22.9 us
    unnamed x4, local copies, waits for them, and re-layouts  2.26 us

profile of v6, /device:TPU:0, one launch (start us, length us, event | category | flops | bytes accessed | tf_op | source)
XLA Modules:
  0.0 25.8 jit_solution(12709081614624144984)
XLA Ops:
  0.6 22.9 %shard_map.86 = (f32[64,512]{1,0:T(8,128)}, f32[16,2048]{1,0:T(8,128)}) custom-call(bf16[16,2048]{1,0:T(8,128)(2,1)} %field.1, bf16[128,512]{1,0:T(8,128)(2,1)} %cot.1, bf16[32,128,128]{2,1,0:T(8,128)(2,1)} %bitcast.1, s32[1,32]{1,0:T(1,128)} %tile_rows.1, s32[8,32]{1,0:T(8,128)} %tile_cols.1, s32[2]{0:T(128)} %lags.1, f32[3,128]{1,0:T(4,128)} %ar_coef.1), custom_call_target="tpu_custom_call" | custom-call | flops 268435456 | bytes 2097152 | tf_op jit(solution)/shard_map/pallas_call | solution.py:320
  23.5 0.0 copy-start
  23.5 1.6 %copy.11 = f32[64,512]{1,0:T(8,128)} copy(f32[64,512]{1,0:T(8,128)} %get-tuple-element.4) | data formatting | bytes 262144
  25.1 0.0 copy-done
  25.1 0.7 %copy.12 = f32[16,2048]{1,0:T(8,128)} copy(f32[16,2048]{1,0:T(8,128)S(1)} %copy-done) | data formatting | bytes 262144
Async XLA Ops:
  23.5 1.6 %copy-start = (f32[16,2048]{1,0:T(8,128)S(1)}, f32[16,2048]{1,0:T(8,128)}, u32[]{:S(2)}) copy-start(f32[16,2048]{1,0:T(8,128)} %get-tuple-element.5) | copy-start | bytes 393220
